TPU v7x, 32 devices: a whole 2x2x4 slice. The times are simulated.
32 devices in a mesh: gx: 4 (over z), gy: 8 (over y, x, core).
Axes of the slice: x: 2, y: 2, z: 4, core: 2. Of those that a mesh axis runs over, the one named last changes fastest.
Arguments:
- seismic: float32 [512, 512, 256], P('gx', 'gy'), may hold values from -41 to 41, as said below
Outputs:
- shift_field: float32 [512, 512, 256], P('gx', 'gy')
- residual: float32 [512, 512, 256], P('gx', 'gy')
Inputs may be any that keep to these rules, and one draw needn't show every extreme that they name: `seismic`: recorded amplitudes of the window.
All inputs are finite; a program needn't handle non-finite values.
Results may differ from a plain program's by a relative error of at most 0.0003.
Values sent between devices are 32-bit elements; how exact they have to be, the bound alone decides.
A program may use at most 320 MiB of HBM per device.

v0:
```python
import jax
import jax.numpy as jnp
from jax import lax
from jax.sharding import PartitionSpec as P

NX = 512
NY = 512
ITERS = 2
damping = 0.001
floor_term = 0.5
highest = lax.Precision.HIGHEST


def extended(block, sides, width):
    for axis, dim in sides:
        count = lax.axis_size(axis)
        forward = [(i, i + 1) for i in range(count - 1)]
        backward = [(target, source) for source, target in forward]
        low = lax.ppermute(
            lax.slice_in_dim(block, block.shape[dim] - width, None, axis=dim), axis, forward
        )
        high = lax.ppermute(lax.slice_in_dim(block, 0, width, axis=dim), axis, backward)
        block = jnp.concatenate([low, block, high], axis=dim)
    return block


def cut(field, start, stop, axis):
    return lax.slice_in_dim(field, start, stop, axis=axis)


def smooth_axis(field, axis):
    length = field.shape[axis]
    return 0.25 * (
        cut(field, 0, length - 2, axis)
        + 2.0 * cut(field, 1, length - 1, axis)
        + cut(field, 2, length, axis)
    )


def pad_time(field):
    return jnp.pad(field, ((0, 0), (0, 0), (1, 1)))


def smooth_all(field):
    return smooth_axis(pad_time(smooth_axis(smooth_axis(field, 0), 1)), 2)


def tensor_fields(padded, inside_x, inside_y):
    mask = inside_x[:, None, None] * inside_y[None, :, None]
    grad_x = 0.5 * (padded[2:, 1:-1] - padded[:-2, 1:-1]) * mask
    grad_y = 0.5 * (padded[1:-1, 2:] - padded[1:-1, :-2]) * mask
    timed = pad_time(padded[1:-1, 1:-1])
    grad_t = 0.5 * (timed[:, :, 2:] - timed[:, :, :-2]) * mask
    cross_x = smooth_all(grad_x * grad_t)
    cross_y = smooth_all(grad_y * grad_t)
    along_t = smooth_all(grad_t * grad_t) + floor_term
    spread = smooth_all(grad_x * grad_x + grad_y * grad_y)
    return (-cross_x / along_t, -cross_y / along_t, along_t / (along_t + spread))


def cosine_table(order):
    freq = jnp.arange(order, dtype=jnp.float32)[:, None]
    place = jnp.arange(order, dtype=jnp.float32)[None, :]
    scale = jnp.where(freq == 0.0, jnp.sqrt(1.0 / order), jnp.sqrt(2.0 / order)).astype(jnp.float32)
    return scale * jnp.cos(jnp.pi * (place + 0.5) * freq / order)


def eigen_values(order):
    freq = jnp.arange(order, dtype=jnp.float32)
    return 2.0 - 2.0 * jnp.cos(jnp.pi * freq / order)


def combine_terms(field, upper_x, lower_x, upper_y, lower_y, weight_x, weight_y, prior_x, prior_y):
    return (
        damping * field
        + weight_x * (field - upper_x)
        + prior_x * (field - lower_x)
        + weight_y * (field - upper_y)
        + prior_y * (field - lower_y)
    )


def operate(field, weight_x, weight_y, prior_x, prior_y):
    padded = extended(field, (("gx", 0), ("gy", 1)), 1)
    return combine_terms(
        field,
        padded[2:, 1:-1],
        padded[:-2, 1:-1],
        padded[1:-1, 2:],
        padded[1:-1, :-2],
        weight_x,
        weight_y,
        prior_x,
        prior_y,
    )


def solve_front(front, table_x, table_y, plane_denom):
    hat = jnp.einsum("ki,tij->tkj", table_x, front, precision=highest)
    hat = jnp.einsum("lj,tkj->tkl", table_y, hat, precision=highest)
    hat = hat / plane_denom
    hat = jnp.einsum("lj,tkl->tkj", table_y, hat, precision=highest)
    return jnp.einsum("ki,tkj->tij", table_x, hat, precision=highest)


def slice_solve(whole, table_x, table_y, plane_denom):
    front = jnp.transpose(whole, (2, 0, 1))
    return jnp.transpose(solve_front(front, table_x, table_y, plane_denom), (1, 2, 0))


def reorder_back(back, rows_x, rows_y, parts_x, parts_y, depth):
    per = depth // (parts_x * parts_y)
    target = jnp.arange(depth, dtype=jnp.int32)
    outer = target // (parts_y * per)
    middle = target // per % parts_y
    source = middle * (parts_x * per) + outer * per + target % per
    select = (jnp.arange(depth, dtype=jnp.int32)[:, None] == source[None, :]).astype(jnp.float32)
    flat = back.reshape(rows_x * rows_y, depth)
    return jnp.dot(flat, select, precision=highest, preferred_element_type=jnp.float32).reshape(
        rows_x, rows_y, depth
    )


def inner(first, second):
    return lax.psum(jnp.sum(first * second), ("gx", "gy"))


def solve(rhs, apply_op, precondition):
    shift_field = jnp.zeros_like(rhs)
    residual = rhs
    precond = precondition(residual)
    direction = precond
    norm_now = inner(residual, precond)
    for step in range(ITERS):
        image = apply_op(direction)
        alpha = norm_now / lax.psum(jnp.sum(direction * image), ("gx", "gy"))
        shift_field = shift_field + alpha * direction
        residual = residual - alpha * image
        if step + 1 < ITERS:
            precond = precondition(residual)
            norm_next = inner(residual, precond)
            direction = precond + norm_next / norm_now * direction
            norm_now = norm_next
    return (shift_field, residual)


def per_device(seismic):
    rows_x, rows_y, depth = seismic.shape
    parts_x = lax.axis_size("gx")
    parts_y = lax.axis_size("gy")
    base_x = lax.axis_index("gx") * rows_x
    base_y = lax.axis_index("gy") * rows_y
    table_x = cosine_table(NX)
    table_y = cosine_table(NY)
    eigen_x = eigen_values(NX)
    eigen_y = eigen_values(NY)
    plane_denom = damping + eigen_x[:, None] + eigen_y[None, :]
    padded = extended(seismic, (("gx", 0), ("gy", 1)), 3)
    grid_x = base_x + jnp.arange(-2, rows_x + 2, dtype=jnp.int32)
    grid_y = base_y + jnp.arange(-2, rows_y + 2, dtype=jnp.int32)
    inside_x = ((grid_x >= 0) & (grid_x < NX)).astype(jnp.float32)
    inside_y = ((grid_y >= 0) & (grid_y < NY)).astype(jnp.float32)
    dip_x, dip_y, weight = tensor_fields(padded, inside_x, inside_y)
    edge_x = grid_x[1:-1]
    edge_y = grid_y[1:-1]
    keep_x = ((edge_x >= 0) & (edge_x < NX - 1)).astype(jnp.float32)
    keep_y = ((edge_y >= 0) & (edge_y < NY - 1)).astype(jnp.float32)
    weight_x = weight * keep_x[:, None, None]
    weight_y = weight * keep_y[None, :, None]
    flux_x = weight_x * dip_x
    flux_y = weight_y * dip_y
    rhs = flux_x[:-2, 1:-1] - flux_x[1:-1, 1:-1] + (flux_y[1:-1, :-2] - flux_y[1:-1, 1:-1])
    own_x = weight_x[1:-1, 1:-1]
    prior_x = weight_x[:-2, 1:-1]
    own_y = weight_y[1:-1, 1:-1]
    prior_y = weight_y[1:-1, :-2]

    def precondition(field):
        whole = lax.all_to_all(
            lax.all_to_all(field, "gx", split_axis=2, concat_axis=0, tiled=True),
            "gy",
            split_axis=2,
            concat_axis=1,
            tiled=True,
        )
        hat = slice_solve(whole, table_x, table_y, plane_denom)
        back = lax.all_to_all(
            lax.all_to_all(hat, "gx", split_axis=0, concat_axis=2, tiled=True),
            "gy",
            split_axis=1,
            concat_axis=2,
            tiled=True,
        )
        return reorder_back(back, rows_x, rows_y, parts_x, parts_y, depth)

    def apply_tiles(field):
        return operate(field, own_x, own_y, prior_x, prior_y)

    return solve(rhs, apply_tiles, precondition)


def solution(mesh):
    placed = (P("gx", "gy", None),)
    return jax.shard_map(
        per_device,
        mesh=mesh,
        in_specs=placed,
        out_specs=(P("gx", "gy", None), P("gx", "gy", None)),
        check_vma=False,
    )
```

profile of v0, /device:TPU:0, one launch (start us, length us, event | category | flops | bytes accessed | tf_op | source)
XLA Modules:
  0.0 2077.2 jit_solution(1720866723027973175)
XLA Ops:
  0.6 8.2 copy.195
  12.4 4.9 collective-permute-start
  18.8 4.1 collective-permute-done
  22.8 4.1 collective-permute-done.1
  34.8 3.8 pad_maximum_fusion
  42.4 4.6 slice.298
  47.0 54.0 %fusion.77 = (f32[132,68,256]{2,0,1:T(8,128)}, f32[132,68,256]{2,0,1:T(8,128)}, f32[132,68,256]{2,0,1:T(8,128)}, f32[132,68,256]{2,0,1:T(8,128)}) fusion(f32[132,68]{0,1:T(8,128)S(1)} %multiply_multiply_fusion, f32[134,70,256]{2,0,1:T(8,128)} %copy-done.2, f32[132,68,256]{2,0,1:T(8,128)} %slice.298), kind=kLoop, calls=%fused_computation.146 | loop fusion | flops 36765696 | bytes 82758720 | tf_op jit(solution)/shard_map/mul | solution.py:55
  101.0 29.4 %fusion.6 = (f32[130,68,256]{2,0,1:T(8,128)}, f32[130,68,256]{2,0,1:T(8,128)}) fusion(f32[132,68,256]{2,0,1:T(8,128)} %get-tuple-element.29, f32[132,68,256]{2,0,1:T(8,128)} %get-tuple-element.30), kind=kLoop, calls=%fused_computation.23 | loop fusion | flops 18104320 | bytes 72417280 | tf_op jit(solution)/shard_map/mul | solution.py:33
  130.3 13.7 broadcast_multiply_fusion.4
  145.2 5.0 broadcast_multiply_fusion.5
  150.2 29.4 %fusion.2 = (f32[130,68,256]{2,0,1:T(8,128)}, f32[130,68,256]{2,0,1:T(8,128)}) fusion(f32[132,68,256]{2,0,1:T(8,128)} %get-tuple-element.27, f32[132,68,256]{2,0,1:T(8,128)} %get-tuple-element.28), kind=kLoop, calls=%fused_computation.15 | loop fusion | flops 18104320 | bytes 72417280 | tf_op jit(solution)/shard_map/mul | solution.py:33
  179.6 13.8 broadcast_multiply_fusion.3
  194.5 5.4 broadcast_multiply_fusion.2
  203.3 45.0 %fusion.24 = (f32[130,66,256]{2,0,1:T(8,128)}, f32[130,66,256]{2,0,1:T(8,128)}, f32[130,66,256]{2,0,1:T(8,128)}, f32[130,66,256]{2,0,1:T(8,128)}) fusion(f32[130,66,256]{2,0,1:T(8,128)} %broadcast_multiply_fusion.3, f32[130,68,256]{2,0,1:T(8,128)} %get-tuple-element.46, f32[130]{0:T(256)S(1)} %and_convert_fusion.1, f32[130,68,256]{2,0,1:T(8,128)S(1)} %bitcast.93, ...), kind=kLoop, calls=%fused_computation.47 | loop fusion | flops 61501440 | bytes 140575232 | tf_op jit(solution)/shard_map/mul | solution.py:170
  248.3 26.7 %fusion.30 = (f32[130,66,256]{2,0,1:T(8,128)}, f32[130,66,256]{2,0,1:T(8,128)}) fusion(f32[130,66,256]{2,0,1:T(8,128)} %get-tuple-element.24, f32[130,66,256]{2,0,1:T(8,128)} %broadcast_multiply_fusion.2, f32[130,68,256]{2,0,1:T(8,128)} %get-tuple-element.45, f32[130,66,256]{2,0,1:T(8,128)} %get-tuple-element.23, f32[66]{0:T(128)S(1)} %copy-done.9), kind=kLoop, calls=%fused_computation.53 | loop fusion | flops 24161280 | bytes 70287624 | tf_op jit(solution)/shard_map/mul | solution.py:171
  275.0 16.4 fusion.59
  291.3 8.7 copy.198
  300.0 185.5 %all_to_all.138 = f32[128,64,256]{0,1,2:T(8,128)S(1)} all-to-all(f32[128,64,256]{0,1,2:T(8,128)} %copy.198), channel_id=1, replica_groups=mesh['gx'=4,'gy'=8] {'gx'}, dimensions={2} | all-to-all | bytes 16777216 | tf_op jit(solution)/shard_map/all_to_all | solution.py:180
  485.5 4.5 copy.275
  490.0 11.4 all-to-all-start.1
  501.6 94.0 %all-to-all-done.1 = f32[512,64,64]{0,1,2:T(8,128)} async-done(((f32[512,64,64]{0,1,2:T(8,128)}), f32[512,64,64]{0,1,2:T(8,128)}, u32[]{:S(2)}, u32[]{:S(2)}) %all-to-all-start.1) | async-done | bytes 8388640 | tf_op jit(solution)/shard_map/all_to_all | solution.py:179
  595.6 8.1 copy.203
  603.7 22.6 %fusion.66 = f32[8,512,512]{2,1,0:T(8,128)S(1)} fusion(f32[512,512,8]{0,2,1:T(8,128)S(1)} %bitcast.102, f32[512]{0:T(512)S(1)} %get-tuple-element.49, f32[512]{0:T(512)S(1)} %get-tuple-element.50), kind=kOutput, calls=%fused_computation.117 | convolution fusion | flops 12885688320 | bytes 16781312 | tf_op jit(solution)/shard_map/ki,tij->tkj/dot_general | solution.py:99
  626.3 34.1 %fusion.64 = f32[8,512,512]{2,1,0:T(8,128)S(1)} fusion(f32[8,512,512]{2,1,0:T(8,128)S(1)} %fusion.66, f32[512]{0:T(512)S(1)} %get-tuple-element.49, f32[512]{0:T(512)S(1)} %get-tuple-element.50), kind=kOutput, calls=%fused_computation.115 | convolution fusion | flops 12885688320 | bytes 16781312 | tf_op jit(solution)/shard_map/lj,tkj->tkl/dot_general | solution.py:100
  660.4 19.8 fusion.72
  680.2 23.2 %convolution_bitcast_fusion.1 = f32[512,512,8]{0,1,2:T(8,128)} fusion(f32[8,512,512]{1,2,0:T(8,128)S(1)} %fusion.72, f32[512]{0:T(512)S(1)} %get-tuple-element.49, f32[512]{0:T(512)S(1)} %get-tuple-element.50), kind=kOutput, calls=%fused_computation.144 | convolution fusion | flops 12885688320 | bytes 16781312 | tf_op jit(solution)/shard_map/ki,tkj->tij/dot_general | solution.py:103
  703.4 10.5 copy.207
  713.9 184.9 %all_to_all.139 = f32[512,512,8]{1,2,0:T(8,128)S(1)} all-to-all(f32[512,512,8]{1,2,0:T(8,128)} %copy.207), channel_id=1, replica_groups=mesh['gx'=4,'gy'=8] {'gx'}, dimensions={0} | all-to-all | bytes 16777216 | tf_op jit(solution)/shard_map/all_to_all | solution.py:188
  898.8 4.4 copy.277
  903.2 11.0 copy.209
  914.3 5.0 all-to-all-start.3
  919.2 94.1 %all-to-all-done.3 = f32[128,512,32]{0,2,1:T(8,128)} async-done(((f32[128,512,32]{0,2,1:T(8,128)}), f32[128,512,32]{0,2,1:T(8,128)}, u32[]{:S(2)}, u32[]{:S(2)}) %all-to-all-start.3) | async-done | bytes 8388640 | tf_op jit(solution)/shard_map/all_to_all | solution.py:187
  1013.3 12.3 copy.210
  1025.6 14.7 reshape.169
  1040.3 9.4 fusion.111
  1051.0 5.0 collective-permute-start.5
  1056.0 4.9 copy.211
  1069.4 36.8 %multiply_reduce_fusion.2 = (f32[]{:T(128)}, f32[]{:T(128)}, f32[128,64,256]{2,0,1:T(8,128)}) fusion(f32[128,64,256]{2,1,0:T(8,128)} %bitcast.97, f32[128,64,256]{2,0,1:T(8,128)} %fusion.59, f32[128,64,256]{2,0,1:T(8,128)} %copy-done.7, f32[1,64,256]{2,0,1:T(1,128)S(1)} %copy.214, f32[1,64,256]{2,0,1:T(1,128)S(1)} %copy.216, ...), kind=kLoop, calls=%fused_computation.131 | loop fusion | flops 52428800 | bytes 67506184 | tf_op jit(solution)/shard_map/reduce_sum | solution.py:136
  1106.2 41.2 %all-reduce.5 = (f32[]{:T(128)}, f32[]{:T(128)}) all-reduce(f32[]{:T(128)} %get-tuple-element.15, f32[]{:T(128)} %get-tuple-element.14), channel_id=1, replica_groups=mesh['gx'=4,'gy'=8] {'gx','gy'}, use_global_device_ids=true, to_apply=%region_1.2 | all-reduce | flops 2 | bytes 16 | tf_op jit(solution)/shard_map/psum | solution.py:125
  1148.7 11.6 multiply_subtract_fusion.1
  1160.3 8.7 copy.226
  1169.1 186.9 %all_to_all.140 = f32[128,64,256]{0,1,2:T(8,128)S(1)} all-to-all(f32[128,64,256]{0,1,2:T(8,128)} %copy.226), channel_id=1, replica_groups=mesh['gx'=4,'gy'=8] {'gx'}, dimensions={2} | all-to-all | bytes 16777216 | tf_op jit(solution)/shard_map/all_to_all | solution.py:180
  1357.0 97.9 %all_to_all.141 = f32[512,64,64]{0,1,2:T(8,128)} all-to-all(f32[512,64,64]{0,1,2:T(8,128)S(1)} %bitcast.109), channel_id=1, replica_groups=mesh['gx'=4,'gy'=8] {'gy'}, dimensions={2} | all-to-all | bytes 16777216 | tf_op jit(solution)/shard_map/all_to_all | solution.py:179
  1455.0 8.1 copy.231
  1463.1 22.6 %fusion.62 = f32[8,512,512]{2,1,0:T(8,128)S(1)} fusion(f32[512,512,8]{0,2,1:T(8,128)S(1)} %bitcast.103, f32[512]{0:T(512)S(1)} %get-tuple-element.49, f32[512]{0:T(512)S(1)} %get-tuple-element.50), kind=kOutput, calls=%fused_computation.113 | convolution fusion | flops 12885688320 | bytes 16781312 | tf_op jit(solution)/shard_map/ki,tij->tkj/dot_general | solution.py:99
  1485.7 34.1 %fusion.60 = f32[8,512,512]{2,1,0:T(8,128)S(1)} fusion(f32[8,512,512]{2,1,0:T(8,128)S(1)} %fusion.62, f32[512]{0:T(512)S(1)} %get-tuple-element.49, f32[512]{0:T(512)S(1)} %get-tuple-element.50), kind=kOutput, calls=%fused_computation.111 | convolution fusion | flops 12885688320 | bytes 16781312 | tf_op jit(solution)/shard_map/lj,tkj->tkl/dot_general | solution.py:100
  1519.8 19.8 fusion.70
  1539.6 23.2 %convolution_bitcast_fusion = f32[512,512,8]{0,1,2:T(8,128)} fusion(f32[8,512,512]{1,2,0:T(8,128)S(1)} %fusion.70, f32[512]{0:T(512)S(1)} %get-tuple-element.49, f32[512]{0:T(512)S(1)} %get-tuple-element.50), kind=kOutput, calls=%fused_computation.143 | convolution fusion | flops 12885688320 | bytes 16781312 | tf_op jit(solution)/shard_map/ki,tkj->tij/dot_general | solution.py:103
  1562.8 10.4 copy.235
  1573.3 187.0 %all_to_all.142 = f32[512,512,8]{1,2,0:T(8,128)S(1)} all-to-all(f32[512,512,8]{1,2,0:T(8,128)} %copy.235), channel_id=1, replica_groups=mesh['gx'=4,'gy'=8] {'gx'}, dimensions={0} | all-to-all | bytes 16777216 | tf_op jit(solution)/shard_map/all_to_all | solution.py:188
  1760.2 4.3 copy.276
  1764.5 11.0 copy.237
  1775.5 97.8 %all_to_all.143 = f32[128,512,32]{0,2,1:T(8,128)S(1)} all-to-all(f32[128,512,32]{0,2,1:T(8,128)} %copy.237), channel_id=1, replica_groups=mesh['gx'=4,'gy'=8] {'gy'}, dimensions={1} | all-to-all | bytes 16777216 | tf_op jit(solution)/shard_map/all_to_all | solution.py:187
  1873.3 5.3 copy.238
  1879.8 14.6 multiply_reduce_fusion.1
  1894.3 38.5 %psum.30 = f32[]{:T(128)} all-reduce(f32[]{:T(128)} %get-tuple-element.43), channel_id=1, replica_groups=mesh['gx'=4,'gy'=8] {'gx','gy'}, use_global_device_ids=true, to_apply=%region_5.6 | all-reduce | flops 1 | bytes 8 | tf_op jit(solution)/shard_map/psum | solution.py:125
  1934.2 14.2 multiply_add_fusion.2
  1951.3 4.5 collective-permute-start.9
  1964.1 20.2 multiply_reduce_fusion
  1984.3 45.3 %psum.31 = f32[]{:T(128)} all-reduce(f32[]{:T(128)} %get-tuple-element.18), channel_id=1, replica_groups=mesh['gx'=4,'gy'=8] {'gx','gy'}, use_global_device_ids=true, to_apply=%region_7.8 | all-reduce | flops 1 | bytes 8 | tf_op jit(solution)/shard_map/psum | solution.py:136
  2030.9 14.2 multiply_add_fusion.1
  2045.1 11.6 multiply_subtract_fusion
  2056.7 12.0 copy.242
  2068.7 8.3 copy.241
  (78 shorter events, 45.6 us)
Async XLA Ops:
  8.9 3.4 copy-start.5
  12.4 10.5 collective-permute-start
  17.3 9.7 collective-permute-start.1
  18.7 16.2 copy-start.6
  28.2 3.8 collective-permute-start.2
  29.5 5.4 collective-permute-start.3
  38.7 3.7 copy-start.2
  130.3 14.9 copy-start
  179.6 14.9 copy-start.1
  179.6 20.3 slice-start
  179.6 20.3 slice-start.1
  179.6 21.7 %slice-start.3 = ((s8[9469952]{0:T(1024)(128)(4,1)}), s8[4194304]{0:T(1024)(128)(4,1)S(1)}, s32[]{:S(2)}) async-start(s8[9469952]{0:T(1024)(128)(4,1)} %bitcast.94), calls=%async_computation.11 | async-start | bytes 8388608
  179.6 22.9 %slice-start.4 = ((s8[9469952]{0:T(1024)(128)(4,1)}), s8[4194304]{0:T(1024)(128)(4,1)S(1)}, s32[]{:S(2)}) async-start(s8[9469952]{0:T(1024)(128)(4,1)} %bitcast.94), calls=%async_computation.12 | async-start | bytes 8388608
  194.5 8.5 slice-start.2
  194.5 8.8 slice-start.5
  203.3 45.0 %copy-start.9 = (f32[66]{0:T(128)S(1)}, f32[66]{0:T(128)}, u32[]{:S(2)}) copy-start(f32[66]{0:T(128)} %and_convert_fusion) | copy-start | bytes 796
  490.0 105.6 %all-to-all-start.1 = ((f32[512,64,64]{0,1,2:T(8,128)}), f32[512,64,64]{0,1,2:T(8,128)}, u32[]{:S(2)}, u32[]{:S(2)}) async-start(f32[512,64,64]{0,1,2:T(8,128)} %bitcast.104), calls=%async_computation.1 | async-start | bytes 16777216 | tf_op jit(solution)/shard_map/all_to_all | solution.py:179
  914.3 99.0 %all-to-all-start.3 = ((f32[128,512,32]{0,2,1:T(8,128)}), f32[128,512,32]{0,2,1:T(8,128)}, u32[]{:S(2)}, u32[]{:S(2)}) async-start(f32[128,512,32]{0,2,1:T(8,128)} %copy.209), calls=%async_computation.3 | async-start | bytes 16777216 | tf_op jit(solution)/shard_map/all_to_all | solution.py:187
  1049.7 11.4 copy-start.3
  1049.7 11.1 collective-permute-start.4
  1051.0 9.9 collective-permute-start.5
  1060.9 3.3 copy-start.7
  1064.1 4.3 collective-permute-start.6
  1065.4 4.0 collective-permute-start.7
  1873.3 5.3 slice-start.6
  1873.3 6.5 slice-start.7
  1948.3 15.8 copy-start.4
  1949.8 6.4 collective-permute-start.8
  1951.3 6.4 collective-permute-start.9
  1958.8 4.3 collective-permute-start.10
  1960.1 4.0 collective-permute-start.11
  2056.7 12.0 copy-start.8
where the time goes:
time: 2080 us
  blocking collectives  1060 us (51%)
  other arithmetic  354 us (17%)
  matrix products  223 us (11%)
  waiting for transfers between devices  203 us (10%)
  local copies, waits for them, and re-layouts  180 us (9%)
  starting transfers between devices  46.8 us (2%)
    all_to_all x2, blocking collectives, precondition(): lax.all_to_all(field, 'gx', split_axis=2, concat_axis=0, tiled=True)  372 us
    all_to_all x2, blocking collectives, precondition(): lax.all_to_all(hat, 'gx', split_axis=0, concat_axis=2, tiled=True)  372 us
    all_to_all x1, blocking collectives, precondition(): lax.all_to_all(lax.all_to_all(field, 'gx', split_axis=2, concat_axis=0, t...  97.9 us
    all_to_all x1, blocking collectives, precondition(): lax.all_to_all(lax.all_to_all(hat, 'gx', split_axis=0, concat_axis=2, til...  97.8 us
    mul x6, other arithmetic, smooth_axis(): 0.25 * (cut(field, 0, length - 2, axis) + 2.0 * cut(field, 1, length - 1,...  96.6 us
    all_to_all x1, waiting for transfers between devices, precondition(): lax.all_to_all(lax.all_to_all(hat, 'gx', split_axis=0, concat_axis=2, til...  94.1 us
    all_to_all x1, waiting for transfers between devices, precondition(): lax.all_to_all(lax.all_to_all(field, 'gx', split_axis=2, concat_axis=0, t...  94 us
    psum x2, blocking collectives, inner(): return lax.psum(jnp.sum(first * second), ('gx', 'gy'))  79.7 us
  transfers between devices with their start and end apart: 14, of which 9 were waited for; matrix products, arithmetic and copies ran while one was open for 0% of the time, Pallas kernels for 0%

commit v1 on v0

--- a/solution.py
+++ b/solution.py
@@ -9,6 +9,13 @@
 damping = 0.001
 floor_term = 0.5
 highest = lax.Precision.HIGHEST
+
+
+def obtain_stages_all_for(arr, dim_no, dim_k):
+    r1 = jnp.concatenate(
+        lax.all_to_all(jnp.stack(jnp.split(arr, lax.axis_size("gx"), dim_no)), "gx", 0, 0), dim_k
+    )
+    return r1
 
 
 def extended(block, sides, width):
@@ -177,11 +184,7 @@
 
     def precondition(field):
         whole = lax.all_to_all(
-            lax.all_to_all(field, "gx", split_axis=2, concat_axis=0, tiled=True),
-            "gy",
-            split_axis=2,
-            concat_axis=1,
-            tiled=True,
+            obtain_stages_all_for(field, 2, 0), "gy", split_axis=2, concat_axis=1, tiled=True
         )
         hat = slice_solve(whole, table_x, table_y, plane_denom)
         back = lax.all_to_all(

time: 2080 us -> 2170 us (1.043)
  local copies, waits for them, and re-layouts: 180 us -> 234 us
    reshape x0 -> x4, local copies, waits for them, and re-layouts: none -> 44.8 us  [obtain_stages_all_for(): jnp.concatenate(lax.all_to_all(jnp.stack(jnp.split(arr, lax.axis_size('gx...]
    another operation x0 -> x4, local copies, waits for them, and re-layouts: none -> 37.4 us  [obtain_stages_all_for(): jnp.stack(jnp.split(arr, lax.axis_size('gx'), dim_no))]
    unnamed x39 -> x41, local copies, waits for them, and re-layouts: 45.5 us -> 44.5 us
where the time goes in v1:
time: 2170 us; the launch traced here: 2160 us
  blocking collectives  1070 us (49%)
  other arithmetic  375 us (17%)
  local copies, waits for them, and re-layouts  234 us (11%)
  matrix products  223 us (10%)
  waiting for transfers between devices  203 us (9%)
  starting transfers between devices  46.8 us (2%)
    all_to_all x2, blocking collectives, obtain_stages_all_for(): lax.all_to_all(jnp.stack(jnp.split(arr, lax.axis_size('gx'), dim_no)), 'g...  379 us
    all_to_all x2, blocking collectives, precondition(): lax.all_to_all(hat, 'gx', split_axis=0, concat_axis=2, tiled=True)  372 us
    all_to_all x1, blocking collectives, precondition(): lax.all_to_all(lax.all_to_all(hat, 'gx', split_axis=0, concat_axis=2, til...  98.1 us
    all_to_all x1, blocking collectives, precondition(): lax.all_to_all(obtain_stages_all_for(field, 2, 0), 'gy', split_axis=2, co...  98 us
    mul x6, other arithmetic, smooth_axis(): 0.25 * (cut(field, 0, length - 2, axis) + 2.0 * cut(field, 1, length - 1,...  96.5 us
    all_to_all x1, waiting for transfers between devices, precondition(): lax.all_to_all(lax.all_to_all(hat, 'gx', split_axis=0, concat_axis=2, til...  94.1 us
    all_to_all x1, waiting for transfers between devices, precondition(): lax.all_to_all(obtain_stages_all_for(field, 2, 0), 'gy', split_axis=2, co...  93.6 us
    psum x2, blocking collectives, inner(): return lax.psum(jnp.sum(first * second), ('gx', 'gy'))  80.1 us
  transfers between devices with their start and end apart: 14, of which 9 were waited for; matrix products, arithmetic and copies ran while one was open for 0% of the time, Pallas kernels for 0%

profile of v1, /device:TPU:0, one launch (start us, length us, event | category | flops | bytes accessed | tf_op | source)
XLA Modules:
  0.0 2159.2 jit_solution(3872489984283521950)
XLA Ops:
  0.6 8.2 copy.187
  12.4 4.9 collective-permute-start
  42.4 4.6 slice.298
  47.0 53.6 %fusion.77 = (f32[132,68,256]{2,0,1:T(8,128)}, f32[132,68,256]{2,0,1:T(8,128)}, f32[132,68,256]{2,0,1:T(8,128)}, f32[132,68,256]{2,0,1:T(8,128)}) fusion(f32[132,68]{0,1:T(8,128)S(1)} %multiply_multiply_fusion, f32[134,70,256]{2,0,1:T(8,128)} %copy-done.2, f32[132,68,256]{2,0,1:T(8,128)} %slice.298), kind=kLoop, calls=%fused_computation.154 | loop fusion | flops 36765696 | bytes 82758720 | tf_op jit(solution)/shard_map/mul | solution.py:62
  100.6 29.3 %fusion.6 = (f32[130,68,256]{2,0,1:T(8,128)}, f32[130,68,256]{2,0,1:T(8,128)}) fusion(f32[132,68,256]{2,0,1:T(8,128)} %get-tuple-element.29, f32[132,68,256]{2,0,1:T(8,128)} %get-tuple-element.30), kind=kLoop, calls=%fused_computation.25 | loop fusion | flops 18104320 | bytes 72417280 | tf_op jit(solution)/shard_map/mul | solution.py:40
  129.9 13.7 broadcast_multiply_fusion.4
  144.8 5.0 broadcast_multiply_fusion.5
  149.8 29.4 %fusion.2 = (f32[130,68,256]{2,0,1:T(8,128)}, f32[130,68,256]{2,0,1:T(8,128)}) fusion(f32[132,68,256]{2,0,1:T(8,128)} %get-tuple-element.27, f32[132,68,256]{2,0,1:T(8,128)} %get-tuple-element.28), kind=kLoop, calls=%fused_computation.17 | loop fusion | flops 18104320 | bytes 72417280 | tf_op jit(solution)/shard_map/mul | solution.py:40
  179.2 13.7 broadcast_multiply_fusion.3
  194.1 5.4 broadcast_multiply_fusion.2
  202.9 55.1 %fusion.24 = (f32[130,66,256]{2,0,1:T(8,128)}, f32[130,66,256]{2,0,1:T(8,128)}, f32[130,66,256]{2,0,1:T(8,128)}, f32[130,66,256]{2,0,1:T(8,128)}) fusion(f32[130,66,256]{2,0,1:T(8,128)} %broadcast_multiply_fusion.3, f32[130,68,256]{2,0,1:T(8,128)} %get-tuple-element.54, f32[130]{0:T(256)S(1)} %and_convert_fusion.1, f32[130,68,256]{2,0,1:T(8,128)S(1)} %bitcast.99, ...), kind=kLoop, calls=%fused_computation.49 | loop fusion | flops 61501440 | bytes 140575232 | tf_op jit(solution)/shard_map/mul | solution.py:177
  258.0 26.8 %fusion.30 = (f32[130,66,256]{2,0,1:T(8,128)}, f32[130,66,256]{2,0,1:T(8,128)}) fusion(f32[130,66,256]{2,0,1:T(8,128)} %get-tuple-element.24, f32[130,66,256]{2,0,1:T(8,128)} %broadcast_multiply_fusion.2, f32[130,68,256]{2,0,1:T(8,128)} %get-tuple-element.53, f32[130,66,256]{2,0,1:T(8,128)} %get-tuple-element.23, f32[66]{0:T(128)S(1)} %copy-done.10), kind=kLoop, calls=%fused_computation.55 | loop fusion | flops 24161280 | bytes 70287624 | tf_op jit(solution)/shard_map/mul | solution.py:178
  284.8 13.4 fusion.59
  298.2 4.7 slice_bitcast_fusion.7
  302.9 8.1 pad_maximum_fusion
  311.0 12.7 copy.190
  323.6 188.9 %all_to_all.112 = f32[4,128,64,64]{1,3,2,0:T(8,128)} all-to-all(f32[4,128,64,64]{1,3,2,0:T(8,128)} %copy.190), channel_id=1, replica_groups=mesh['gx'=4,'gy'=8] {'gx'}, dimensions={0} | all-to-all | bytes 16777216 | tf_op jit(solution)/shard_map/all_to_all | solution.py:16
  512.5 12.2 copy.238
  524.7 10.3 reshape.181
  534.9 11.8 all-to-all-start.1
  547.0 93.6 %all-to-all-done.1 = f32[512,64,64]{0,1,2:T(8,128)} async-done(((f32[512,64,64]{0,1,2:T(8,128)}), f32[512,64,64]{0,1,2:T(8,128)}, u32[]{:S(2)}, u32[]{:S(2)}) %all-to-all-start.1) | async-done | bytes 8388640 | tf_op jit(solution)/shard_map/all_to_all | solution.py:186
  640.6 8.1 copy.194
  648.7 22.4 %fusion.66 = f32[8,512,512]{2,1,0:T(8,128)S(1)} fusion(f32[512,512,8]{0,2,1:T(8,128)S(1)} %bitcast.108, f32[512]{0:T(512)S(1)} %get-tuple-element.57, f32[512]{0:T(512)S(1)} %get-tuple-element.58), kind=kOutput, calls=%fused_computation.117 | convolution fusion | flops 12885688320 | bytes 16781312 | tf_op jit(solution)/shard_map/ki,tij->tkj/dot_general | solution.py:106
  671.0 34.1 %fusion.64 = f32[8,512,512]{2,1,0:T(8,128)S(1)} fusion(f32[8,512,512]{2,1,0:T(8,128)S(1)} %fusion.66, f32[512]{0:T(512)S(1)} %get-tuple-element.57, f32[512]{0:T(512)S(1)} %get-tuple-element.58), kind=kOutput, calls=%fused_computation.115 | convolution fusion | flops 12885688320 | bytes 16781312 | tf_op jit(solution)/shard_map/lj,tkj->tkl/dot_general | solution.py:107
  705.2 19.8 fusion.72
  725.0 23.4 %convolution_bitcast_fusion.1 = f32[512,512,8]{0,1,2:T(8,128)} fusion(f32[8,512,512]{1,2,0:T(8,128)S(1)} %fusion.72, f32[512]{0:T(512)S(1)} %get-tuple-element.57, f32[512]{0:T(512)S(1)} %get-tuple-element.58), kind=kOutput, calls=%fused_computation.152 | convolution fusion | flops 12885688320 | bytes 16781312 | tf_op jit(solution)/shard_map/ki,tkj->tij/dot_general | solution.py:110
  748.4 10.5 copy.198
  758.9 184.8 %all_to_all.113 = f32[512,512,8]{1,2,0:T(8,128)S(1)} all-to-all(f32[512,512,8]{1,2,0:T(8,128)} %copy.198), channel_id=1, replica_groups=mesh['gx'=4,'gy'=8] {'gx'}, dimensions={0} | all-to-all | bytes 16777216 | tf_op jit(solution)/shard_map/all_to_all | solution.py:191
  948.2 11.0 copy.200
  959.2 5.0 all-to-all-start.3
  964.2 94.1 %all-to-all-done.3 = f32[128,512,32]{0,2,1:T(8,128)} async-done(((f32[128,512,32]{0,2,1:T(8,128)}), f32[128,512,32]{0,2,1:T(8,128)}, u32[]{:S(2)}, u32[]{:S(2)}) %all-to-all-start.3) | async-done | bytes 8388640 | tf_op jit(solution)/shard_map/all_to_all | solution.py:190
  1058.3 12.3 copy.201
  1070.6 14.7 reshape.176
  1085.3 9.4 fusion.111
  1096.0 4.8 collective-permute-start.5
  1100.8 4.9 copy.202
  1114.3 36.8 %multiply_reduce_fusion.2 = (f32[]{:T(128)}, f32[]{:T(128)}, f32[128,64,256]{2,0,1:T(8,128)}) fusion(f32[128,64,256]{2,1,0:T(8,128)} %bitcast.103, f32[128,64,256]{2,0,1:T(8,128)} %copy-done.4, f32[128,64,256]{2,0,1:T(8,128)} %copy-done.8, f32[1,64,256]{2,0,1:T(1,128)S(1)} %copy.205, f32[1,64,256]{2,0,1:T(1,128)S(1)} %copy.207, ...), kind=kLoop, calls=%fused_computation.131 | loop fusion | flops 52428800 | bytes 67506184 | tf_op jit(solution)/shard_map/reduce_sum | solution.py:143
  1151.1 41.6 %all-reduce.5 = (f32[]{:T(128)}, f32[]{:T(128)}) all-reduce(f32[]{:T(128)} %get-tuple-element.15, f32[]{:T(128)} %get-tuple-element.14), channel_id=1, replica_groups=mesh['gx'=4,'gy'=8] {'gx','gy'}, use_global_device_ids=true, to_apply=%region_1.2 | all-reduce | flops 2 | bytes 16 | tf_op jit(solution)/shard_map/psum | solution.py:132
  1193.9 11.6 multiply_subtract_fusion.1
  1205.5 7.4 slice_bitcast_fusion.3
  1212.9 6.2 pad_maximum_fusion.1
  1219.1 12.7 copy.217
  1231.7 190.2 %all_to_all.114 = f32[4,128,64,64]{1,3,2,0:T(8,128)} all-to-all(f32[4,128,64,64]{1,3,2,0:T(8,128)} %copy.217), channel_id=1, replica_groups=mesh['gx'=4,'gy'=8] {'gx'}, dimensions={0} | all-to-all | bytes 16777216 | tf_op jit(solution)/shard_map/all_to_all | solution.py:16
  1422.0 12.0 copy.240
  1434.0 10.4 reshape.182
  1444.4 98.0 %all_to_all.115 = f32[512,64,64]{0,1,2:T(8,128)S(1)} all-to-all(f32[512,64,64]{0,1,2:T(8,128)} %reshape.182), channel_id=1, replica_groups=mesh['gx'=4,'gy'=8] {'gy'}, dimensions={2} | all-to-all | bytes 16777216 | tf_op jit(solution)/shard_map/all_to_all | solution.py:186
  1542.4 4.9 copy.221
  1547.2 22.6 %fusion.62 = f32[8,512,512]{2,1,0:T(8,128)S(1)} fusion(f32[512,512,8]{0,2,1:T(8,128)S(1)} %bitcast.109, f32[512]{0:T(512)S(1)} %get-tuple-element.57, f32[512]{0:T(512)S(1)} %get-tuple-element.58), kind=kOutput, calls=%fused_computation.113 | convolution fusion | flops 12885688320 | bytes 16781312 | tf_op jit(solution)/shard_map/ki,tij->tkj/dot_general | solution.py:106
  1569.8 34.1 %fusion.60 = f32[8,512,512]{2,1,0:T(8,128)S(1)} fusion(f32[8,512,512]{2,1,0:T(8,128)S(1)} %fusion.62, f32[512]{0:T(512)S(1)} %get-tuple-element.57, f32[512]{0:T(512)S(1)} %get-tuple-element.58), kind=kOutput, calls=%fused_computation.111 | convolution fusion | flops 12885688320 | bytes 16781312 | tf_op jit(solution)/shard_map/lj,tkj->tkl/dot_general | solution.py:107
  1604.0 19.8 fusion.70
  1623.8 23.2 %convolution_bitcast_fusion = f32[512,512,8]{0,1,2:T(8,128)} fusion(f32[8,512,512]{1,2,0:T(8,128)S(1)} %fusion.70, f32[512]{0:T(512)S(1)} %get-tuple-element.57, f32[512]{0:T(512)S(1)} %get-tuple-element.58), kind=kOutput, calls=%fused_computation.151 | convolution fusion | flops 12885688320 | bytes 16781312 | tf_op jit(solution)/shard_map/ki,tkj->tij/dot_general | solution.py:110
  1647.0 10.4 copy.225
  1657.4 187.0 %all_to_all.116 = f32[512,512,8]{1,2,0:T(8,128)S(1)} all-to-all(f32[512,512,8]{1,2,0:T(8,128)} %copy.225), channel_id=1, replica_groups=mesh['gx'=4,'gy'=8] {'gx'}, dimensions={0} | all-to-all | bytes 16777216 | tf_op jit(solution)/shard_map/all_to_all | solution.py:191
  1848.7 11.0 copy.227
  1859.6 98.1 %all_to_all.117 = f32[128,512,32]{0,2,1:T(8,128)S(1)} all-to-all(f32[128,512,32]{0,2,1:T(8,128)} %copy.227), channel_id=1, replica_groups=mesh['gx'=4,'gy'=8] {'gy'}, dimensions={1} | all-to-all | bytes 16777216 | tf_op jit(solution)/shard_map/all_to_all | solution.py:190
  1962.0 14.6 multiply_reduce_fusion.1
  1976.6 38.5 %psum.30 = f32[]{:T(128)} all-reduce(f32[]{:T(128)} %get-tuple-element.51), channel_id=1, replica_groups=mesh['gx'=4,'gy'=8] {'gx','gy'}, use_global_device_ids=true, to_apply=%region_5.6 | all-reduce | flops 1 | bytes 8 | tf_op jit(solution)/shard_map/psum | solution.py:132
  2016.3 14.2 multiply_add_fusion.2
  2046.2 20.2 multiply_reduce_fusion
  2066.4 45.2 %psum.31 = f32[]{:T(128)} all-reduce(f32[]{:T(128)} %get-tuple-element.18), channel_id=1, replica_groups=mesh['gx'=4,'gy'=8] {'gx','gy'}, use_global_device_ids=true, to_apply=%region_7.8 | all-reduce | flops 1 | bytes 8 | tf_op jit(solution)/shard_map/psum | solution.py:143
  2112.9 14.2 multiply_add_fusion.1
  2127.1 11.6 multiply_subtract_fusion
  2138.7 12.0 copy.232
  2150.7 8.3 copy.231
  (86 shorter events, 73.2 us)
Async XLA Ops:
  8.9 3.4 copy-start.6
  12.4 10.5 collective-permute-start
  17.3 9.7 collective-permute-start.1
  18.7 16.2 copy-start.7
  28.2 3.7 collective-permute-start.2
  29.5 5.4 collective-permute-start.3
  38.7 3.8 copy-start.2
  129.9 14.9 copy-start
  179.2 14.9 copy-start.1
  179.2 20.3 slice-start
  179.2 20.3 slice-start.1
  179.2 21.7 %slice-start.3 = ((s8[9469952]{0:T(1024)(128)(4,1)}), s8[4194304]{0:T(1024)(128)(4,1)S(1)}, s32[]{:S(2)}) async-start(s8[9469952]{0:T(1024)(128)(4,1)} %bitcast.100), calls=%async_computation.11 | async-start | bytes 8388608
  179.2 22.9 %slice-start.4 = ((s8[9469952]{0:T(1024)(128)(4,1)}), s8[4194304]{0:T(1024)(128)(4,1)S(1)}, s32[]{:S(2)}) async-start(s8[9469952]{0:T(1024)(128)(4,1)} %bitcast.100), calls=%async_computation.12 | async-start | bytes 8388608
  194.1 8.5 slice-start.2
  194.1 8.8 slice-start.5
  202.9 55.1 %copy-start.10 = (f32[66]{0:T(128)S(1)}, f32[66]{0:T(128)}, u32[]{:S(2)}) copy-start(f32[66]{0:T(128)} %and_convert_fusion) | copy-start | bytes 796
  298.2 4.7 copy-start.4
  534.9 105.6 %all-to-all-start.1 = ((f32[512,64,64]{0,1,2:T(8,128)}), f32[512,64,64]{0,1,2:T(8,128)}, u32[]{:S(2)}, u32[]{:S(2)}) async-start(f32[512,64,64]{0,1,2:T(8,128)} %reshape.181), calls=%async_computation.1 | async-start | bytes 16777216 | tf_op jit(solution)/shard_map/all_to_all | solution.py:186
  959.2 99.0 %all-to-all-start.3 = ((f32[128,512,32]{0,2,1:T(8,128)}), f32[128,512,32]{0,2,1:T(8,128)}, u32[]{:S(2)}, u32[]{:S(2)}) async-start(f32[128,512,32]{0,2,1:T(8,128)} %copy.200), calls=%async_computation.3 | async-start | bytes 16777216 | tf_op jit(solution)/shard_map/all_to_all | solution.py:190
  1094.7 11.0 copy-start.3
  1094.7 11.0 collective-permute-start.4
  1096.0 9.7 collective-permute-start.5
  1105.7 3.3 copy-start.8
  1109.0 4.3 collective-permute-start.6
  1110.3 4.0 collective-permute-start.7
  1859.6 102.4 %slice-start.6 = ((s8[8388608]{0:T(1024)(128)(4,1)}), s8[4194304]{0:T(1024)(128)(4,1)S(1)}, s32[]{:S(2)}) async-start(s8[8388608]{0:T(1024)(128)(4,1)} %bitcast.106), calls=%async_computation.14 | async-start | bytes 8388608
  1957.7 4.4 slice-start.7
  2030.5 15.8 copy-start.5
  2031.9 6.4 collective-permute-start.8
  2033.5 6.4 collective-permute-start.9
  2040.9 4.3 collective-permute-start.10
  2042.2 4.0 collective-permute-start.11
  2138.7 12.0 copy-start.9
